TPU v7x, 128 devices: a whole 4x4x4 slice. The times are simulated.
128 devices in a mesh: heads: 4 (over y), seq: 32 (over x, z, core).
Axes of the slice: x: 4, y: 4, z: 4, core: 2. Of those that a mesh axis runs over, the one named last changes fastest.
Arguments:
- inputs: bfloat16 [32768, 2048], P('seq', 'heads'), may hold values from -6 to 6
- w_query: bfloat16 [2048, 2048], P(None, 'heads'), may hold values from -0.125 to 0.125
- w_key: bfloat16 [2048, 2048], P(None, 'heads'), may hold values from -0.125 to 0.125
- w_value: bfloat16 [2048, 2048], P(None, 'heads'), may hold values from -0.125 to 0.125
- w_out: bfloat16 [2048, 2048], P('heads'), may hold values from -0.125 to 0.125
- beta_code: int32 [32768, 16], P('seq', 'heads'), may hold values from 1 to 128, as said below
- gain: float32 [128], replicated, may hold values from 0.5 to 1.5
Outputs:
- mixed: float32 [32768, 2048], P(('seq', 'heads'))
Inputs may be any that keep to these rules, and one draw needn't show every extreme that they name: beta_code / 64 lies in (0, 2], the range of the negative-eigenvalue variant of DeltaNet.
All inputs are finite; a program needn't handle non-finite values.
Results may differ from a plain program's by a relative error of at most 0.0034.
Values may be sent and summed in bfloat16 or wider, within the bound.
A program may use at most 128 MiB of HBM per device.

v0:
```python
import jax
import jax.numpy as jnp
from jax import lax
from jax.sharding import PartitionSpec as P

DK = 128
C = 64


def passed_along(x, axis, by):
    size = lax.axis_size(axis)
    pairs = [(i, i + by) for i in range(size) if 0 <= i + by < size]
    return lax.ppermute(x, axis, pairs)


def unit_norm(field):
    return field * lax.rsqrt(jnp.sum(field * field, -1, keepdims=True) + 1e-06)


def local(inputs, w_query, w_key, w_value, w_out, beta_code, gain):
    highest_level = lax.Precision.HIGHEST
    tokens = inputs.shape[0]
    width = w_query.shape[1]
    groups = width // DK
    blocks = tokens // C
    piece = lax.all_gather(inputs, "heads", axis=1, tiled=True)
    query, keys, values = tuple(
        (
            jnp.dot(piece, weight, preferred_element_type=jnp.float32)
            for weight in (w_query, w_key, w_value)
        )
    )

    def split_point(field):
        return field.reshape(blocks, C, groups, DK).transpose(0, 2, 1, 3)

    q_blocks = split_point(unit_norm(query.reshape(tokens, groups, DK)))
    k_blocks = split_point(unit_norm(keys.reshape(tokens, groups, DK)))
    v_blocks = split_point(values.reshape(tokens, groups, DK))
    strength = beta_code.astype(jnp.float32) / 64.0
    b_blocks = strength.reshape(blocks, C, groups).transpose(0, 2, 1)
    ident = jnp.eye(C, dtype=jnp.float32)
    strict = jnp.tril(jnp.ones((C, C), jnp.float32), -1)
    inclusive = jnp.tril(jnp.ones((C, C), jnp.float32), 0)
    inner = jnp.einsum("nhik,nhjk->nhij", k_blocks, k_blocks, precision=highest_level)
    lower = ident + strict * (b_blocks[..., None] * inner)
    right = b_blocks[..., None] * jnp.concatenate([k_blocks, v_blocks], -1)
    solved = jax.scipy.linalg.solve_triangular(lower, right, lower=True, unit_diagonal=True)
    w_mats = solved[..., :DK]
    u_mats = solved[..., DK:]
    scores = inclusive * jnp.einsum("nhik,nhjk->nhij", q_blocks, k_blocks, precision=highest_level)
    eye_state = jnp.broadcast_to(jnp.eye(DK, dtype=jnp.float32), (groups, DK, DK))
    transfers = eye_state - jnp.einsum("nhik,nhil->nhkl", k_blocks, w_mats, precision=highest_level)
    zero_state = jnp.zeros((groups, DK, DK), jnp.float32)

    def gather_effect(carry, item):
        running_total, running_state = carry
        key_block, weight_block, update_block, trans_b = item
        fresh_state = update_block - jnp.einsum(
            "znt,ztc->znc", weight_block, running_state, precision=highest_level
        )
        running_state = running_state + jnp.einsum(
            "pwc,pwq->pcq", key_block, fresh_state, precision=highest_level
        )
        running_total = jnp.einsum("hkl,hlm->hkm", trans_b, running_total, precision=highest_level)
        return ((running_total, running_state), None)

    (running_total, shard_local_state), _ = lax.scan(
        gather_effect, (eye_state, zero_state), (k_blocks, w_mats, u_mats, transfers)
    )

    def relay(turn, carry):
        outgoing_state, incoming_state = carry
        incoming_state = passed_along(outgoing_state, "seq", 1)
        outgoing_state = (
            jnp.einsum("dtc,dcm->dtm", running_total, incoming_state, precision=highest_level)
            + shard_local_state
        )
        return (outgoing_state, incoming_state)

    _, start_state = lax.fori_loop(
        0, lax.axis_size("seq") - 1, relay, (shard_local_state, zero_state)
    )

    def emit(running_state, item):
        query_block, key_block, weight_block, update_block, score_b = item
        fresh_state = update_block - jnp.einsum(
            "znt,ztc->znc", weight_block, running_state, precision=highest_level
        )
        layer_result = jnp.einsum(
            "znt,ztc->znc", query_block, running_state, precision=highest_level
        )
        layer_result = layer_result + jnp.einsum(
            "hij,hjv->hiv", score_b, fresh_state, precision=highest_level
        )
        running_state = running_state + jnp.einsum(
            "pwc,pwq->pcq", key_block, fresh_state, precision=highest_level
        )
        return (running_state, layer_result)

    _, outputs = lax.scan(emit, start_state, (q_blocks, k_blocks, w_mats, u_mats, scores))
    outputs = outputs.transpose(0, 2, 1, 3).reshape(tokens, groups, DK)
    scale = lax.rsqrt(jnp.mean(outputs * outputs, -1, keepdims=True) + 1e-06)
    normed = (outputs * scale * gain).astype(jnp.bfloat16).reshape(tokens, width)
    return lax.psum_scatter(
        jnp.dot(normed, w_out, preferred_element_type=jnp.float32),
        "heads",
        scatter_dimension=0,
        tiled=True,
    )


def solution(mesh):
    in_specs = (
        P("seq", "heads"),
        P(None, "heads"),
        P(None, "heads"),
        P(None, "heads"),
        P("heads", None),
        P("seq", "heads"),
        P(),
    )
    out_specs = P(("seq", "heads"), None)
    return jax.shard_map(local, mesh=mesh, in_specs=in_specs, out_specs=out_specs, check_vma=False)
```

profile of v0, /device:TPU:6, one launch (start us, length us, event | category | flops | bytes accessed | tf_op | source)
XLA Modules:
  0.0 1054.6 jit_solution(11085783315219309148)
XLA Ops:
  11.7 48.0 %all-gather.2.cloned.1.call-done = bf16[1024,2048]{1,0:T(8,128)(2,1)} async-done(((bf16[1024,512]{1,0:T(8,128)(2,1)}), bf16[1024,2048]{1,0:T(8,128)(2,1)}) %all-gather.2.cloned.1.call-update) | async-done | bytes 4194320 | tf_op jit(solution)/shard_map/all_gather | solution.py:26
  99.1 316.0 %custom-call.4 = f32[16,4,1,64,64]{3,4,2,1,0:T(8,128)} custom-call(f32[16,4,1,64,64]{4,3,2,1,0:T(8,128)} %add_bitcast_fusion), custom_call_target="InvertDiagBlocksLowerTriangular" | custom-call | tf_op jit(solution)/shard_map/jit(_solve_triangular)/vmap(vmap())/triangular_solve | solution.py:48
  435.4 8.2 convolution_subtract_fusion.2
  443.6 68.5 %while.39 = (s32[]{:T(128)}, f32[4,128,128]{2,1,0:T(8,128)S(1)}, f32[4,128,128]{2,1,0:T(8,128)S(1)}, f32[16,4,128,128]{3,2,1,0:T(8,128)}, f32[16,4,64,128]{3,2,1...) while((s32[]{:T(128)}, f32[4,128,128]{2,1,0:T(8,128)S(1)}, ...), condition=%wide.region_2.3_spmd.clone, body=%wide.region_1.0_spmd.clone.sunk | while | flops 201555968 | bytes 2754664 | solution.py:68
  520.3 325.6 %while.37 = (s32[]{:T(128)}, f32[4,128,128]{2,1,0:T(8,128)S(1)}, f32[4,128,128]{2,1,0:T(8,128)}, f32[4,128,128]{2,1,0:T(8,128)S(1)}, f32[4,128,128]{2,1,0:T(8,128)S(1)}, /*index=5*/s32[]{:T(128)}) while((s32[]{:T(128)}, f32[4,128,128]{2,1,0:T(8,128)S(1)}, f32[4,128,128]{2,1,0:T(8,128)}, f32[4,128,128]{2,1,0:T(8,128)S(1)}, ...), condition=%wide.region_4.5_spmd, body=%wide.region_3.4_spmd.sunk | while | flops 100728832 | bytes 3145865 | solution.py:81
  522.2 7.9 collective-permute-done
  532.7 7.9 collective-permute-done
  543.2 7.9 collective-permute-done
  553.7 7.9 collective-permute-done
  564.2 7.9 collective-permute-done
  574.7 7.9 collective-permute-done
  585.2 7.9 collective-permute-done
  595.7 7.9 collective-permute-done
  606.2 7.9 collective-permute-done
  616.7 7.9 collective-permute-done
  627.2 7.9 collective-permute-done
  637.7 7.9 collective-permute-done
  648.2 7.9 collective-permute-done
  732.3 7.9 collective-permute-done
  742.8 7.9 collective-permute-done
  826.8 7.9 collective-permute-done
  837.3 7.9 collective-permute-done
  845.9 111.1 %while.38 = (s32[]{:T(128)}, f32[4,128,128]{2,1,0:T(8,128)}, f32[16,4,64,128]{3,2,1,0:T(8,128)}, f32[16,4,64,128]{3,2,1,0:T(8,128)}, f32[16,4,64,128]{3,2,1,0:T(...) while((s32[]{:T(128)}, f32[4,128,128]{2,1,0:T(8,128)}, ...), condition=%wide.region_7.8_spmd, body=%wide.region_6.7_spmd.sunk | while | flops 176291840 | bytes 2493533 | solution.py:101
  969.4 78.4 %reduce-scatter.2.cloned.1.call-done = f32[256,2048]{1,0:T(8,128)} async-done(((f32[1024,2048]{1,0:T(8,128)}), f32[256,2048]{1,0:T(8,128)}) %reduce-scatter.2.cloned.1.call-update) | async-done | bytes 2097168 | tf_op jit(solution)/shard_map/reduce_scatter | solution.py:105
  (334 shorter events, 454.8 us)
Async XLA Ops:
  6.5 53.1 %all-gather.2.cloned.1.call-start = ((), (), s32[]{:S(2)}) async-start(), calls=%async_computation.1 | async-start | bytes 5242880 | tf_op jit(solution)/shard_map/all_gather | solution.py:26
  7.3 1040.5 %reduce-scatter.2.cloned.1.call-start = ((), (), s32[]{:S(2)}) async-start(), calls=%async_computation.2 | async-start | bytes 10485760 | tf_op jit(solution)/shard_map/reduce_scatter | solution.py:105
  520.3 9.8 collective-permute-start
  530.8 9.8 collective-permute-start
  541.3 9.8 collective-permute-start
  551.8 9.8 collective-permute-start
  562.3 9.8 collective-permute-start
  572.8 9.8 collective-permute-start
  583.3 9.8 collective-permute-start
  593.8 9.8 collective-permute-start
  604.3 9.8 collective-permute-start
  614.8 9.8 collective-permute-start
  625.3 9.8 collective-permute-start
  635.8 9.8 collective-permute-start
  646.3 9.8 collective-permute-start
  656.8 9.8 collective-permute-start
  667.3 9.8 collective-permute-start
  677.8 9.8 collective-permute-start
  688.3 9.8 collective-permute-start
  698.8 9.8 collective-permute-start
  709.4 9.8 collective-permute-start
  719.9 9.8 collective-permute-start
  730.4 9.8 collective-permute-start
  740.9 9.8 collective-permute-start
  (51 other events, 1092.0 us)
Sparse Core Ops, SparseCore 0:
  9.0 50.5 all-gather.1
  969.5 78.2 reduce-scatter.1
where the time goes:
time: 1060 us; the launch traced here: 1050 us
  waiting for transfers between devices  371 us (35%)
  other arithmetic  331 us (31%)
  matrix products  238 us (22%)
  starting transfers between devices  59.2 us (6%)
  local copies, waits for them, and re-layouts  39.9 us (4%)
  between operations  13.6 us (1%)
    another operation x4, other arithmetic, local(): jax.scipy.linalg.solve_triangular(lower, right, lower=True, unit_diagonal...  317 us
    ppermute x31, waiting for transfers between devices, passed_along(): return lax.ppermute(x, axis, pairs)  244 us
    reduce_scatter x1, waiting for transfers between devices, local(): lax.psum_scatter(jnp.dot(normed, w_out, preferred_element_type=jnp.float3...  78.4 us
    ppermute x31, starting transfers between devices, passed_along(): return lax.ppermute(x, axis, pairs)  59.2 us
    all_gather x1, waiting for transfers between devices, local(): piece = lax.all_gather(inputs, 'heads', axis=1, tiled=True)  48 us
    dot_general x16, matrix products, emit(): jnp.einsum('pwc,pwq->pcq', key_block, fresh_state, precision=highest_level)  37.3 us
    dot_general x16, matrix products, emit(): jnp.einsum('znt,ztc->znc', query_block, running_state, precision=highest_...  32.5 us
    dot_general x16, matrix products, gather_effect(): jnp.einsum('pwc,pwq->pcq', key_block, fresh_state, precision=highest_level)  24.4 us
  transfers between devices with their start and end apart: 33, of which 33 were waited for; matrix products, arithmetic and copies ran while one was open for 0% of the time, Pallas kernels for 0%

commit v1 on v0

v1 whole, which is shorter than its diff:
```python
import functools

import jax
import jax.numpy as jnp
from jax import lax
from jax.experimental import pallas as pl
from jax.experimental.pallas import tpu as pltpu
from jax.sharding import PartitionSpec as P

DK = 128
BLOCK = 128
CHUNK = 256
F32 = jnp.float32
BF16 = jnp.bfloat16


def halves(a):
    high = a.astype(BF16)
    return high, (a - high.astype(F32)).astype(BF16)


def dot(a, b):
    return jnp.dot(a, b, preferred_element_type=F32)


def product_narrow(a, b):
    left = jnp.concatenate(halves(a), 1)
    right = jnp.concatenate(halves(b), 1)
    both = dot(left, jnp.concatenate([right, right], 0))
    return both[:, :DK] + both[:, DK:]


def product_wide(a, b):
    a_high, a_low = halves(a)
    b_high, b_low = halves(b)
    first = dot(jnp.concatenate([a_high, a_low], 1), jnp.concatenate([b_high, b_high], 0))
    return first + dot(a_high, b_low)


def unit_norm(field):
    return field * lax.rsqrt(jnp.sum(field * field, -1, keepdims=True) + 1e-06)


def scan_kernel(x_ref, wq_ref, wk_ref, wv_ref, b_ref, state_in, o_ref, state_out):
    parts, rows, depth = x_ref.shape
    groups = wq_ref.shape[1] // DK

    def project(w_ref):
        total = dot(x_ref[0], w_ref[pl.ds(0, depth), :])
        for part in range(1, parts):
            total += dot(x_ref[part], w_ref[pl.ds(part * depth, depth), :])
        return total

    query, keys, values = project(wq_ref), project(wk_ref), project(wv_ref)
    strength = b_ref[...].astype(F32) * (1.0 / 64.0)
    row = lax.broadcasted_iota(jnp.int32, (BLOCK, BLOCK), 0)
    col = lax.broadcasted_iota(jnp.int32, (BLOCK, BLOCK), 1)
    ident = (row == col).astype(F32)
    differ = row ^ col
    level = jnp.zeros((BLOCK, BLOCK), jnp.int32)
    for t in range(1, 7):
        level += (differ >= (1 << t)).astype(jnp.int32)
    level = jnp.where(row > col, level, -1)

    items = [(b, h) for b in range(rows // BLOCK) for h in range(groups)]

    def cut(field, b, h):
        return field[b * BLOCK : (b + 1) * BLOCK, h * DK : (h + 1) * DK]

    q = [unit_norm(cut(query, b, h)) for b, h in items]
    k = [unit_norm(cut(keys, b, h)) for b, h in items]
    beta = [strength[b * BLOCK : (b + 1) * BLOCK, h : h + 1] for b, h in items]
    k_turned = [a.T for a in k]
    grams = [product_narrow(jnp.concatenate([a, c], 0), t) for a, c, t in zip(k, q, k_turned)]
    below = [e * g[:BLOCK] for e, g in zip(beta, grams)]
    scores = [jnp.where(row >= col, g[BLOCK:], 0.0) for g in grams]
    inverse = [ident - jnp.where(level == 0, n, 0.0) for n in below]
    for t in range(1, 7):
        inner = [product_narrow(jnp.where(level == t, n, 0.0), x) for n, x in zip(below, inverse)]
        inverse = [x - product_narrow(x, y) for x, y in zip(inverse, inner)]
    uw = [
        product_wide(x, e * jnp.concatenate([cut(values, b, h), a], 1))
        for x, e, a, (b, h) in zip(inverse, beta, k, items)
    ]
    effect = [product_wide(jnp.concatenate([t, s], 0), m) for t, s, m in zip(k_turned, scores, uw)]
    zero = jnp.zeros((BLOCK, DK), F32)
    state = [state_in[h] for h in range(groups)]
    for (b, h), g, a in zip(items, effect, q):
        step = jnp.concatenate([ident - g[:BLOCK, DK:], a - g[BLOCK:, DK:]], 0)
        after = product_wide(step, state[h])
        state[h] = after[:BLOCK] + jnp.concatenate([g[:BLOCK, :DK], zero], 1)
        o_ref[h, pl.ds(b * BLOCK, BLOCK), :] = after[BLOCK:] + jnp.concatenate(
            [g[BLOCK:, :DK], zero], 1
        )
    for h in range(groups):
        state_out[h] = state[h]


def local_scan(x, w_query, w_key, w_value, beta_code, state):
    parts, rows, depth = x.shape
    width = w_query.shape[1]
    groups = width // DK
    return pl.pallas_call(
        scan_kernel,
        out_shape=[
            jax.ShapeDtypeStruct((groups, rows, 2 * DK), F32),
            jax.ShapeDtypeStruct(state.shape, F32),
        ],
        compiler_params=pltpu.CompilerParams(vmem_limit_bytes=48 * 1024 * 1024),
        cost_estimate=pl.CostEstimate(
            flops=2 * rows * 2048 * width * 6, bytes_accessed=8 << 20, transcendentals=0
        ),
    )(x, w_query, w_key, w_value, beta_code, state)


MESH = pl.DeviceIdType.MESH


def chain_kernel(
    end_ref, o_hbm, gain_ref, out_ref,
    sibling_end, totals, prefixes, row_in, row_out, start_out, start_in, starts, o_ref, parcels,
    pair_send, pair_recv, z_send, z_recv, x_send, x_recv, a_send, a_recv, o_sem,
):
    group = lax.axis_index("heads")
    me = lax.axis_index("seq")
    groups = lax.axis_size("heads")
    core, z, x = me % 2, (me // 2) % 4, me // 8
    sibling = me + 1 - 2 * core

    def at(x, z, core):
        return {"seq": x * 8 + z * 2 + core}

    barrier = pltpu.get_barrier_semaphore()

    def greet(where):
        pl.semaphore_signal(barrier, inc=1, device_id=where, device_id_type=MESH)

    o_copy = pltpu.make_async_copy(o_hbm, o_ref, o_sem)
    o_copy.start()
    greet({"seq": sibling})
    for d in range(1, 4):
        greet(at(x, (z + d) % 4, core))
        greet({"heads": (group + d) % groups})
    greet(at((x + 1) % 4, z, core))
    greet(at((x + 3) % 4, z, core))
    pl.semaphore_wait(barrier, 9)

    mine, theirs = 2 * core, 2 - 2 * core
    pair = pltpu.make_async_remote_copy(
        src_ref=end_ref.at[pl.ds(theirs, 2)], dst_ref=sibling_end,
        send_sem=pair_send.at[0], recv_sem=pair_recv.at[0],
        device_id={"seq": sibling}, device_id_type=MESH,
    )
    pair.start()
    zero = jnp.zeros((DK, DK), F32)
    ident = (
        lax.broadcasted_iota(jnp.int32, (DK, DK), 0) == lax.broadcasted_iota(jnp.int32, (DK, DK), 1)
    ).astype(F32)

    def after(second, first):
        return product_wide(second[:, DK:], first) + jnp.concatenate([second[:, :DK], zero], 1)

    pair.wait()
    early = []
    for i in range(2):
        own, other = end_ref[mine + i], sibling_end[i]
        first = jnp.where(core == 0, own, other)
        second = jnp.where(core == 0, other, own)
        early.append(first)
        totals[z, i] = after(second, first)

    copies = []
    for d in (1, 3, 2):
        copies.append(
            pltpu.make_async_remote_copy(
                src_ref=totals.at[z], dst_ref=totals.at[z],
                send_sem=z_send.at[d - 1], recv_sem=z_recv.at[d - 1],
                device_id=at(x, (z + d) % 4, core), device_id_type=MESH,
            )
        )
        copies[-1].start()

    @pl.when(x == 0)
    def _():
        row_in[...] = jnp.zeros_like(row_in)

    for copy in copies:
        copy.wait()

    low = [after(totals[1, i], totals[0, i]) for i in range(2)]
    high = [after(totals[3, i], totals[2, i]) for i in range(2)]
    whole = [after(b, a) for a, b in zip(low, high)]
    hops = [
        pltpu.make_async_remote_copy(
            src_ref=row_out.at[i], dst_ref=row_in.at[i],
            send_sem=x_send.at[i], recv_sem=x_recv.at[i],
            device_id=at((x + 1) % 4, z, core), device_id_type=MESH,
        )
        for i in range(2)
    ]

    def pass_on(i, state):
        row_out[i] = product_narrow(whole[i][:, DK:], state) + whole[i][:, :DK]
        hops[i].start()

    @pl.when(x == 0)
    def _():
        for i in range(2):
            row_out[i] = whole[i][:, :DK]
            hops[i].start()

    for i in range(2):
        prefixes[0, i] = jnp.concatenate([zero, ident], 1)
        prefixes[1, i] = totals[0, i]
        prefixes[2, i] = low[i]
        prefixes[3, i] = after(totals[2, i], low[i])
    heads = [prefixes[z, i] for i in range(2)]
    seconds = [after(early[i], heads[i]) for i in range(2)]

    for i in range(2):
        @pl.when(x > 0)
        def _():
            hops[i].wait_recv()

        @pl.when(jnp.logical_and(x > 0, x < 3))
        def _():
            pass_on(i, row_in[i])

    for i in range(2):
        both = jnp.concatenate([heads[i], seconds[i]], 0)
        state = product_narrow(both[:, DK:], row_in[i]) + both[:, :DK]
        starts[mine + i] = jnp.where(core == 0, state[:DK], state[DK:])
        start_out[i] = jnp.where(core == 0, state[DK:], state[:DK])
    back = pltpu.make_async_remote_copy(
        src_ref=start_out, dst_ref=start_in,
        send_sem=pair_send.at[1], recv_sem=pair_recv.at[1],
        device_id={"seq": sibling}, device_id_type=MESH,
    )
    back.start()
    o_copy.wait()
    back.wait()
    for i in range(2):
        starts[theirs + i] = start_in[i]

    @pl.when(x < 3)
    def _():
        for i in range(2):
            hops[i].wait_send()

    rows = parcels.shape[1]
    sends = []
    gain = gain_ref[...]
    for d in (1, 2, 3, 0):
        quarter = (group + d) % groups
        for g in range(starts.shape[0]):
            piece = o_ref[g, pl.ds(pl.multiple_of(quarter * rows, rows), rows), :]
            o = piece[:, :DK] + product_narrow(piece[:, DK:], starts[g])
            scale = lax.rsqrt(jnp.mean(o * o, -1, keepdims=True) + 1e-06)
            normed = (o * scale * gain).astype(BF16)
            if d == 0:
                out_ref[group, :, g * DK : (g + 1) * DK] = normed
            else:
                parcels[d - 1, :, g * DK : (g + 1) * DK] = normed
        if d > 0:
            sends.append(
                pltpu.make_async_remote_copy(
                    src_ref=parcels.at[d - 1], dst_ref=out_ref.at[group],
                    send_sem=a_send.at[d - 1], recv_sem=a_recv.at[d - 1],
                    device_id={"heads": quarter}, device_id_type=MESH,
                )
            )
            sends[-1].start()
    for copy in sends:
        copy.wait()


def chain(end, o, gain):
    groups, tokens, _ = o.shape
    shares = lax.axis_size("heads")
    rows = tokens // shares
    dma = pltpu.SemaphoreType.DMA
    vmem = pl.BlockSpec(memory_space=pltpu.VMEM)
    return pl.pallas_call(
        chain_kernel,
        out_shape=jax.ShapeDtypeStruct((shares, rows, groups * DK), BF16),
        in_specs=[vmem, pl.BlockSpec(memory_space=pl.ANY), vmem],
        out_specs=vmem,
        scratch_shapes=[
            pltpu.VMEM((2, DK, 2 * DK), F32),
            pltpu.VMEM((4, 2, DK, 2 * DK), F32),
            pltpu.VMEM((4, 2, DK, 2 * DK), F32),
            pltpu.VMEM((2, DK, DK), F32),
            pltpu.VMEM((2, DK, DK), F32),
            pltpu.VMEM((2, DK, DK), F32),
            pltpu.VMEM((2, DK, DK), F32),
            pltpu.VMEM((groups, DK, DK), F32),
            pltpu.VMEM(o.shape, F32),
            pltpu.VMEM((shares - 1, rows, groups * DK), BF16),
            dma((2,)), dma((2,)), dma((3,)), dma((3,)), dma((2,)), dma((2,)), dma((3,)), dma((3,)),
            dma,
        ],
        compiler_params=pltpu.CompilerParams(
            collective_id=0, has_side_effects=True, vmem_limit_bytes=32 * 1024 * 1024
        ),
        cost_estimate=pl.CostEstimate(flops=10**9, bytes_accessed=64 << 20, transcendentals=0),
    )(end, o, gain)


def out_kernel(y_ref, w_ref, out_ref):
    part = dot(y_ref[0], w_ref[0])

    @pl.when(pl.program_id(0) == 0)
    def _():
        out_ref[...] = part

    @pl.when(pl.program_id(0) > 0)
    def _():
        out_ref[...] += part


def project_out(normed, w_out):
    shares, rows, width = normed.shape
    return pl.pallas_call(
        out_kernel,
        grid=(shares,),
        out_shape=jax.ShapeDtypeStruct((rows, w_out.shape[2]), F32),
        in_specs=[
            pl.BlockSpec((1, rows, width), lambda h: (h, 0, 0)),
            pl.BlockSpec((1, width, w_out.shape[2]), lambda h: (h, 0, 0)),
        ],
        out_specs=pl.BlockSpec((rows, w_out.shape[2]), lambda h: (0, 0)),
        compiler_params=pltpu.CompilerParams(vmem_limit_bytes=32 * 1024 * 1024),
    )(normed, w_out)


def whole_w_out(w_out):
    rows = w_out.shape[0] // lax.axis_size("seq")
    share = lax.dynamic_slice_in_dim(w_out, lax.axis_index("seq") * rows, rows, 0)
    across = lax.all_gather(share, "heads", axis=0, tiled=False)
    return lax.all_gather(across, "seq", axis=1, tiled=False).reshape(
        lax.axis_size("heads"), w_out.shape[0], w_out.shape[1]
    )


def local(inputs, w_query, w_key, w_value, w_out, beta_code, gain):
    tokens = inputs.shape[0]
    groups = w_query.shape[1] // DK
    w_whole = whole_w_out(w_out)
    ident = jnp.broadcast_to(jnp.eye(DK, dtype=F32), (groups, DK, DK))
    state = jnp.concatenate([jnp.zeros((groups, DK, DK), F32), ident], 2)
    outs = []
    for start in range(0, tokens, CHUNK):
        part = slice(start, start + CHUNK)
        piece = lax.all_gather(inputs[part], "heads", axis=0, tiled=False)
        o, state = local_scan(piece, w_query, w_key, w_value, beta_code[part], state)
        outs.append(o)
    normed = chain(state, jnp.concatenate(outs, 1), gain.reshape(1, DK))
    return project_out(normed, w_whole)


def solution(mesh):
    in_specs = (
        P("seq", "heads"),
        P(None, "heads"),
        P(None, "heads"),
        P(None, "heads"),
        P("heads", None),
        P("seq", "heads"),
        P(),
    )
    out_specs = P(("seq", "heads"), None)
    return jax.shard_map(local, mesh=mesh, in_specs=in_specs, out_specs=out_specs, check_vma=False)
```

time: 1060 us -> 199 us (0.19)
  other arithmetic: 331 us -> 0.36 us
  waiting for transfers between devices: 371 us -> 46.3 us
  matrix products: 238 us -> 0 us
  Pallas kernels: 0 us -> 94.8 us
  starting transfers between devices: 59.2 us -> 0.16 us
  blocking collectives: 0 us -> 13.5 us
    another operation x4 -> x0, other arithmetic: 317 us -> none  [local(): jax.scipy.linalg.solve_triangular(lower, right, lower=True, unit_diagonal...]
    ppermute x31 -> x0, waiting for transfers between devices: 244 us -> none  [passed_along(): return lax.ppermute(x, axis, pairs)]
    dot_general x150 -> x0, matrix products: 234 us -> none  [the longest x16 37.3 us: emit(): jnp.einsum('pwc,pwq->pcq', key_block, fresh_state, precision=highest_level)]
    pallas_call x0 -> x6, Pallas kernels: none -> 94.8 us  [the longest x1 56.5 us: chain(): pl.pallas_call(chain_kernel, out_shape=jax.ShapeDtypeStruct((shares, rows...]
    reduce_scatter x1 -> x0, waiting for transfers between devices: 78.4 us -> none  [local(): lax.psum_scatter(jnp.dot(normed, w_out, preferred_element_type=jnp.float3...]
    ppermute x31 -> x0, starting transfers between devices: 59.2 us -> none  [passed_along(): return lax.ppermute(x, axis, pairs)]
    unnamed x23 -> x50, local copies, waits for them, and re-layouts: 0.16 us -> 25.5 us
    all_gather x0 -> x1, blocking collectives: none -> 13.5 us  [whole_w_out(): across = lax.all_gather(share, 'heads', axis=0, tiled=False)]
  transfers between devices with their start and end apart: 33 -> 5, of which waited for: 33 -> 4; matrix products, arithmetic and copies ran while one was open for 0% -> 2% of each run, Pallas kernels for 0% -> 45%
where the time goes in v1:
time: 199 us; the launch traced here: 198 us
  Pallas kernels  94.8 us (48%)
  waiting for transfers between devices  46.3 us (23%)
  local copies, waits for them, and re-layouts  29.5 us (15%)
  blocking collectives  13.5 us (7%)
  between operations  13.3 us (7%)
    pallas_call x1, Pallas kernels, chain(): pl.pallas_call(chain_kernel, out_shape=jax.ShapeDtypeStruct((shares, rows...  56.5 us
    all_gather x4, waiting for transfers between devices, local(): piece = lax.all_gather(inputs[part], 'heads', axis=0, tiled=False)  44.3 us
    pallas_call x4, Pallas kernels, local_scan(): pl.pallas_call(scan_kernel, out_shape=[jax.ShapeDtypeStruct((groups, rows...  33.4 us
    unnamed x50, local copies, waits for them, and re-layouts  25.5 us
    all_gather x1, blocking collectives, whole_w_out(): across = lax.all_gather(share, 'heads', axis=0, tiled=False)  13.5 us
    pallas_call x1, Pallas kernels, project_out(): pl.pallas_call(out_kernel, grid=(shares,), out_shape=jax.ShapeDtypeStruct...  4.88 us
  transfers between devices with their start and end apart: 5, of which 4 were waited for; matrix products, arithmetic and copies ran while one was open for 2% of the time, Pallas kernels for 45%

profile of v1, /device:TPU:6, one launch (start us, length us, event | category | flops | bytes accessed | tf_op | source)
XLA Modules:
  0.0 197.9 jit_solution(3250363916584390649)
XLA Ops:
  6.5 2.3 %fusion.1 = (bf16[256,512]{1,0:T(8,128)(2,1)}, bf16[256,512]{1,0:T(8,128)(2,1)}, bf16[256,512]{1,0:T(8,128)(2,1)}, bf16[256,512]{1,0:T(8,128)(2,1)}) fusion(bf16[1024,512]{1,0:T(8,128)(2,1)} %param.7), kind=kLoop, calls=%fused_computation.4 | loop fusion | bytes 2097152 | tf_op jit(solution)/shard_map/slice | solution.py:354
  11.1 13.5 %all-gather.4 = bf16[64,2048]{1,0:T(8,128)(2,1)} all-gather(bf16[16,2048]{1,0:T(8,128)(2,1)S(1)} %constant_dynamic-slice_fusion), channel_id=6, replica_groups=mesh['heads'=4,'seq'=32] {'heads'}, dimensions={0}, use_global_device_ids=true | all-gather | bytes 327680 | tf_op jit(solution)/shard_map/all_gather | solution.py:339
  27.5 7.9 %all-gather.18.cloned.1.call-done = bf16[1024,512]{1,0:T(8,128)(2,1)} async-done(((bf16[256,512]{1,0:T(8,128)(2,1)}), bf16[1024,512]{1,0:T(8,128)(2,1)}) %all-gather.18.cloned.1.call-update) | async-done | bytes 1048592 | tf_op jit(solution)/shard_map/all_gather | solution.py:354
  35.4 1.0 copy-done.6
  37.3 1.6 copy-done.9
  38.9 1.2 copy-done.13
  40.1 8.3 %shard_map.73 = (f32[4,256,256]{2,1,0:T(8,128)S(1)}, f32[4,128,256]{2,1,0:T(8,128)S(1)}) custom-call(bf16[4,256,512]{2,1,0:T(8,128)(2,1)S(1)} %bitcast.7, bf16[2048,512]{1,0:T(8,128)(2,1)S(1)} %copy-done.9, bf16[2048,512]{1,0:T(8,128)(2,1)} %wk_ref.7, bf16[2048,512]{1,0:T(8,128)(2,1)} %wv_ref.7, s32[256,4]{1,0:T(8,128)S(1)} %copy-done.7, ...), custom_call_target="tpu_custom_call" | custom-call | flops 3221225472 | bytes 8388608 | tf_op jit(solution)/shard_map/pallas_call | solution.py:103
  49.2 12.6 %all-gather.16.cloned.1.call-done = bf16[1024,512]{1,0:T(8,128)(2,1)} async-done(((bf16[256,512]{1,0:T(8,128)(2,1)}), bf16[1024,512]{1,0:T(8,128)(2,1)}) %all-gather.16.cloned.1.call-update) | async-done | bytes 1048592 | tf_op jit(solution)/shard_map/all_gather | solution.py:354
  61.8 1.6 copy-done.10
  63.4 1.2 copy-done.14
  65.6 8.3 %shard_map.74 = (f32[4,256,256]{2,1,0:T(8,128)S(1)}, f32[4,128,256]{2,1,0:T(8,128)S(1)}) custom-call(bf16[4,256,512]{2,1,0:T(8,128)(2,1)S(1)} %bitcast.8, bf16[2048,512]{1,0:T(8,128)(2,1)S(1)} %copy-done.10, bf16[2048,512]{1,0:T(8,128)(2,1)} %wk_ref.7, bf16[2048,512]{1,0:T(8,128)(2,1)} %wv_ref.7, s32[256,4]{1,0:T(8,128)S(1)} %copy.14.b_ref, ...), custom_call_target="tpu_custom_call" | custom-call | flops 3221225472 | bytes 8388608 | tf_op jit(solution)/shard_map/pallas_call | solution.py:103
  75.7 12.1 %all-gather.14.cloned.1.call-done = bf16[1024,512]{1,0:T(8,128)(2,1)} async-done(((bf16[256,512]{1,0:T(8,128)(2,1)}), bf16[1024,512]{1,0:T(8,128)(2,1)}) %all-gather.14.cloned.1.call-update) | async-done | bytes 1048592 | tf_op jit(solution)/shard_map/all_gather | solution.py:354
  87.8 1.6 copy-done.11
  89.4 1.2 copy-done.15
  90.6 1.0 copy-done.20
  91.7 8.5 %shard_map.75 = (f32[4,256,256]{2,1,0:T(8,128)S(1)}, f32[4,128,256]{2,1,0:T(8,128)S(1)}) custom-call(bf16[4,256,512]{2,1,0:T(8,128)(2,1)S(1)} %bitcast.9, bf16[2048,512]{1,0:T(8,128)(2,1)S(1)} %copy-done.11, bf16[2048,512]{1,0:T(8,128)(2,1)} %wk_ref.7, bf16[2048,512]{1,0:T(8,128)(2,1)} %wv_ref.7, s32[256,4]{1,0:T(8,128)S(1)} %copy.13.b_ref, ...), custom_call_target="tpu_custom_call" | custom-call | flops 3221225472 | bytes 8388608 | tf_op jit(solution)/shard_map/pallas_call | solution.py:103
  101.9 11.7 %all-gather.12.cloned.1.call-done = bf16[1024,512]{1,0:T(8,128)(2,1)} async-done(((bf16[256,512]{1,0:T(8,128)(2,1)}), bf16[1024,512]{1,0:T(8,128)(2,1)}) %all-gather.12.cloned.1.call-update) | async-done | bytes 1048592 | tf_op jit(solution)/shard_map/all_gather | solution.py:354
  113.6 1.6 copy-done.12
  115.2 1.2 copy-done.16
  116.5 1.0 copy-done.22
  117.5 8.4 %shard_map.76 = (f32[4,256,256]{2,1,0:T(8,128)S(1)}, f32[4,128,256]{2,1,0:T(8,128)S(1)}) custom-call(bf16[4,256,512]{2,1,0:T(8,128)(2,1)S(1)} %bitcast.10, bf16[2048,512]{1,0:T(8,128)(2,1)S(1)} %copy-done.12, bf16[2048,512]{1,0:T(8,128)(2,1)} %wk_ref.7, bf16[2048,512]{1,0:T(8,128)(2,1)} %wv_ref.7, s32[256,4]{1,0:T(8,128)S(1)} %copy.12.b_ref, ...), custom_call_target="tpu_custom_call" | custom-call | flops 3221225472 | bytes 8388608 | tf_op jit(solution)/shard_map/pallas_call | solution.py:103
  126.6 56.5 %shard_map.77.y_ref = bf16[4,256,512]{2,1,0:T(8,128)(2,1)S(1)} custom-call(f32[4,128,256]{2,1,0:T(8,128)S(1)} %get-tuple-element.16.end_ref, f32[4,1024,256]{2,1,0:T(8,128)S(1)} %pad_maximum_fusion.o_hbm, f32[1,128]{1,0:T(1,128)S(1)} %bitcast.6), custom_call_target="tpu_custom_call" | custom-call | flops 1000000000 | bytes 67108864 | tf_op jit(solution)/shard_map/pallas_call | solution.py:283
  183.1 3.4 %copy-done.1 = bf16[4,512,2048]{2,1,0:T(8,128)(2,1)S(1)} copy-done((bf16[4,512,2048]{2,1,0:T(8,128)(2,1)S(1)}, bf16[4,512,2048]{2,1,0:T(8,128)(2,1)}, u32[]{:S(2)}) %copy-start.1) | copy-done | bytes 8388632
  186.5 4.9 %shard_map.78 = f32[256,2048]{1,0:T(8,128)} custom-call(bf16[4,256,512]{2,1,0:T(8,128)(2,1)S(1)} %shard_map.77.y_ref, bf16[4,512,2048]{2,1,0:T(8,128)(2,1)S(1)} %copy-done.1), custom_call_target="tpu_custom_call" | custom-call | tf_op jit(solution)/shard_map/pallas_call | solution.py:323
  (55 shorter events, 11.9 us)
Async XLA Ops:
  6.5 4.5 %copy-start = (bf16[512,2048]{1,0:T(8,128)(2,1)S(1)}, bf16[512,2048]{1,0:T(8,128)(2,1)}, u32[]{:S(2)}) copy-start(bf16[512,2048]{1,0:T(8,128)(2,1)} %param.11) | copy-start | bytes 6291460
  6.5 28.8 %all-gather.18.cloned.1.call-start = ((), (), s32[]{:S(2)}) async-start(), calls=%async_computation.3 | async-start | bytes 1310720 | tf_op jit(solution)/shard_map/all_gather | solution.py:354
  8.9 52.9 %all-gather.16.cloned.1.call-start = ((), (), s32[]{:S(2)}) async-start(), calls=%async_computation.2 | async-start | bytes 1310720 | tf_op jit(solution)/shard_map/all_gather | solution.py:354
  9.7 78.1 %all-gather.14.cloned.1.call-start = ((), (), s32[]{:S(2)}) async-start(), calls=%async_computation.1 | async-start | bytes 1310720 | tf_op jit(solution)/shard_map/all_gather | solution.py:354
  10.4 103.2 %all-gather.12.cloned.1.call-start = ((), (), s32[]{:S(2)}) async-start(), calls=%async_computation | async-start | bytes 1310720 | tf_op jit(solution)/shard_map/all_gather | solution.py:354
  11.0 172.1 %all-gather.20.cloned.1.call-start = ((), (), s32[]{:S(2)}) async-start(), calls=%async_computation.4 | async-start | bytes 8650752 | tf_op jit(solution)/shard_map/all_gather | solution.py:340
  35.4 1.0 copy-start.6
  36.4 0.9 copy-start.7
  37.3 1.6 copy-start.9
  38.9 1.2 copy-start.13
  61.8 1.6 copy-start.10
  63.4 1.2 copy-start.14
  64.6 1.0 copy-start.18
  73.9 1.0 copy-start.2
  87.8 1.6 copy-start.11
  89.4 1.2 copy-start.15
  90.6 1.0 copy-start.20
  100.1 1.0 copy-start.4
  113.6 1.6 copy-start.12
  115.2 1.2 copy-start.16
  116.5 1.0 copy-start.22
  117.5 8.4 %copy-start.3 = (f32[4,256,256]{2,1,0:T(8,128)S(1)}, f32[4,256,256]{2,1,0:T(8,128)}, u32[]{:S(2)}) copy-start(f32[4,256,256]{2,1,0:T(8,128)} %copy-done.2) | copy-start | bytes 3145732
  117.5 8.4 %copy-start.5 = (f32[4,256,256]{2,1,0:T(8,128)S(1)}, f32[4,256,256]{2,1,0:T(8,128)}, u32[]{:S(2)}) copy-start(f32[4,256,256]{2,1,0:T(8,128)} %copy-done.4) | copy-start | bytes 3145732
  183.1 3.4 %copy-start.1 = (bf16[4,512,2048]{2,1,0:T(8,128)(2,1)S(1)}, bf16[4,512,2048]{2,1,0:T(8,128)(2,1)}, u32[]{:S(2)}) copy-start(bf16[4,512,2048]{2,1,0:T(8,128)(2,1)} %all-gather.20.cloned.1.call-done.w_ref) | copy-start | bytes 25165828
  (4 other events, 3.0 us)
Sparse Core Ops, SparseCore 0:
  9.0 26.2 all-gather.17
  37.0 24.7 all-gather.15
  63.5 24.3 all-gather.13
  89.3 24.2 all-gather.11
  115.8 55.8 all-gather.19

commit v2 on v1

v2 whole, which is shorter than its diff:
```python
import functools

import jax
import jax.numpy as jnp
from jax import lax
from jax.experimental import pallas as pl
from jax.experimental.pallas import tpu as pltpu
from jax.sharding import PartitionSpec as P

DK = 128
BLOCK = 128
CHUNK = 256
F32 = jnp.float32
BF16 = jnp.bfloat16


def halves(a):
    high = a.astype(BF16)
    return high, (a - high.astype(F32)).astype(BF16)


def dot(a, b):
    return jnp.dot(a, b, preferred_element_type=F32)


def product_narrow(a, b):
    left = jnp.concatenate(halves(a), 1)
    right = jnp.concatenate(halves(b), 1)
    both = dot(left, jnp.concatenate([right, right], 0))
    return both[:, :DK] + both[:, DK:]


def product_wide(a, b):
    a_high, a_low = halves(a)
    b_high, b_low = halves(b)
    first = dot(jnp.concatenate([a_high, a_low], 1), jnp.concatenate([b_high, b_high], 0))
    return first + dot(a_high, b_low)


def unit_norm(field):
    return field * lax.rsqrt(jnp.sum(field * field, -1, keepdims=True) + 1e-06)


MESH = pl.DeviceIdType.MESH


def iotas():
    return (
        lax.broadcasted_iota(jnp.int32, (BLOCK, BLOCK), 0),
        lax.broadcasted_iota(jnp.int32, (BLOCK, BLOCK), 1),
    )


def scan_chunk(query, keys, values, strength, state_ref, o_ref, start):
    rows, width = query.shape
    groups = width // DK
    row, col = iotas()
    ident = (row == col).astype(F32)
    differ = row ^ col
    level = jnp.zeros((BLOCK, BLOCK), jnp.int32)
    for t in range(1, 7):
        level += (differ >= (1 << t)).astype(jnp.int32)
    level = jnp.where(row > col, level, -1)

    items = [(b, h) for b in range(rows // BLOCK) for h in range(groups)]

    def cut(field, b, h):
        return field[b * BLOCK : (b + 1) * BLOCK, h * DK : (h + 1) * DK]

    q = [unit_norm(cut(query, b, h)) for b, h in items]
    k = [unit_norm(cut(keys, b, h)) for b, h in items]
    beta = [strength[b * BLOCK : (b + 1) * BLOCK, h : h + 1] for b, h in items]
    k_turned = [a.T for a in k]
    grams = [product_narrow(jnp.concatenate([a, c], 0), t) for a, c, t in zip(k, q, k_turned)]
    below = [e * g[:BLOCK] for e, g in zip(beta, grams)]
    scores = [jnp.where(row >= col, g[BLOCK:], 0.0) for g in grams]
    inverse = [ident - jnp.where(level == 0, n, 0.0) for n in below]
    for t in range(1, 7):
        inner = [product_narrow(jnp.where(level == t, n, 0.0), x) for n, x in zip(below, inverse)]
        inverse = [x - product_narrow(x, y) for x, y in zip(inverse, inner)]
    uw = [
        product_wide(x, e * jnp.concatenate([cut(values, b, h), a], 1))
        for x, e, a, (b, h) in zip(inverse, beta, k, items)
    ]
    effect = [product_wide(jnp.concatenate([t, s], 0), m) for t, s, m in zip(k_turned, scores, uw)]
    zero = jnp.zeros((BLOCK, DK), F32)
    state = [state_ref[h] for h in range(groups)]
    for (b, h), g, a in zip(items, effect, q):
        step = jnp.concatenate([ident - g[:BLOCK, DK:], a - g[BLOCK:, DK:]], 0)
        after = product_wide(step, state[h])
        state[h] = after[:BLOCK] + jnp.concatenate([g[:BLOCK, :DK], zero], 1)
        o_ref[h, pl.ds(start + b * BLOCK, BLOCK), :] = after[BLOCK:] + jnp.concatenate(
            [g[BLOCK:, :DK], zero], 1
        )
    for h in range(groups):
        state_ref[h] = state[h]


def layer_kernel(
    x_ref, wq_hbm, wk_hbm, wv_hbm, b_ref, gain_ref, out_ref,
    w_ref, others, end_ref, o_ref,
    sibling_end, totals, row_in, row_out, start_out, start_in, starts, parcels, relays,
    w_sem, g_send, g_recv, f_send, f_recv,
    pair_send, pair_recv, back_send, back_recv, z_send, z_recv, x_send, x_recv,
    a_send, a_recv, r_send, r_recv, p_send, p_recv,
):
    group = lax.axis_index("heads")
    me = lax.axis_index("seq")
    groups = lax.axis_size("heads")
    core, z, x = me % 2, (me // 2) % 4, me // 8
    sibling = me + 1 - 2 * core
    tokens, depth = x_ref.shape
    chunks = tokens // CHUNK
    half = CHUNK // 2

    def at(x, z, core):
        return {"seq": x * 8 + z * 2 + core}

    def beside(d):
        return {"heads": (group + d) % groups}

    def remote(src, dst, send, recv, where):
        return pltpu.make_async_remote_copy(
            src_ref=src, dst_ref=dst, send_sem=send, recv_sem=recv,
            device_id=where, device_id_type=MESH,
        )

    barrier = pltpu.get_barrier_semaphore()

    def greet(where):
        pl.semaphore_signal(barrier, inc=1, device_id=where, device_id_type=MESH)

    greet({"seq": sibling})
    for d in range(1, 4):
        greet(at(x, (z + d) % 4, core))
        greet(beside(d))
    greet(at((x + 1) % 4, z, core))
    greet(at((x + 3) % 4, z, core))
    loads = [
        pltpu.make_async_copy(w, w_ref.at[i], w_sem.at[i])
        for i, w in enumerate((wq_hbm, wk_hbm, wv_hbm))
    ]
    for load in loads:
        load.start()
    pl.semaphore_wait(barrier, 9)

    def direct(c, d):
        rows = pl.ds(pl.multiple_of(c * CHUNK, CHUNK), CHUNK)
        return remote(
            x_ref.at[rows], others.at[d - 1, rows], g_send.at[c, d // 2], g_recv.at[c, d // 2],
            beside(d),
        )

    def onward(c, j):
        rows = pl.ds(pl.multiple_of(c * CHUNK + j * half, half), half)
        return remote(
            others.at[2 * j, rows], others.at[1, rows], f_send.at[c, j], f_recv.at[c, j],
            beside(1 + 2 * j),
        )

    def start_direct(c):
        direct(c, 1).start()
        direct(c, 3).start()

    def start_onward(c):
        direct(c, 1).wait_recv()
        direct(c, 3).wait_recv()
        onward(c, 0).start()
        onward(c, 1).start()

    start_direct(0)
    start_direct(1)
    row, col = iotas()
    ident = (row == col).astype(F32)
    zero = jnp.zeros((DK, DK), F32)
    for h in range(end_ref.shape[0]):
        end_ref[h] = jnp.concatenate([zero, ident], 1)
    start_onward(0)
    start_direct(2)
    for load in loads:
        load.wait()

    def step(c, carry):
        rows = pl.ds(pl.multiple_of(c * CHUNK, CHUNK), CHUNK)

        def part(i, d):
            source = lax.rem(group + groups - d, groups)
            piece = x_ref[rows, :] if d == 0 else others[d - 1, rows, :]
            return dot(piece, w_ref[i, pl.ds(pl.multiple_of(source * depth, depth), depth), :])

        fields = [part(i, 0) + part(i, 1) + part(i, 3) for i in range(3)]
        onward(c, 0).wait_recv()
        onward(c, 1).wait_recv()
        query, keys, values = [f + part(i, 2) for i, f in enumerate(fields)]

        @pl.when(c + 1 < chunks)
        def _():
            start_onward(c + 1)

        @pl.when(c + 3 < chunks)
        def _():
            start_direct(c + 3)

        strength = b_ref[rows, :].astype(F32) * (1.0 / 64.0)
        scan_chunk(
            query, keys, values, strength, end_ref, o_ref, pl.multiple_of(c * CHUNK, CHUNK)
        )
        return carry

    lax.fori_loop(0, chunks, step, 0)

    mine, theirs = 2 * core, 2 - 2 * core

    def after(second, first):
        return product_wide(second[:, DK:], first) + jnp.concatenate([second[:, :DK], zero], 1)

    pairs = [
        remote(
            end_ref.at[theirs + i], sibling_end.at[i], pair_send.at[i], pair_recv.at[i],
            {"seq": sibling},
        )
        for i in range(2)
    ]
    for pair in pairs:
        pair.start()

    @pl.when(x == 0)
    def _():
        row_in[...] = jnp.zeros_like(row_in)

    early = []
    z_copies = []
    for i in range(2):
        pairs[i].wait_recv()
        own, other = end_ref[mine + i], sibling_end[i]
        first = jnp.where(core == 0, own, other)
        second = jnp.where(core == 0, other, own)
        early.append(first)
        totals[i, z] = after(second, first)
        z_copies.append(
            [
                remote(
                    totals.at[i, z], totals.at[i, z], z_send.at[i, d - 1], z_recv.at[i, d - 1],
                    at(x, (z + d) % 4, core),
                )
                for d in (1, 3, 2)
            ]
        )
        for copy in z_copies[i]:
            copy.start()

    hops = [
        remote(
            row_out.at[i], row_in.at[i], x_send.at[i], x_recv.at[i], at((x + 1) % 4, z, core)
        )
        for i in range(2)
    ]

    def pass_on(i, whole):
        @pl.when(x == 0)
        def _():
            row_out[i] = whole[:, :DK]
            hops[i].start()

        @pl.when(jnp.logical_and(x > 0, x < 3))
        def _():
            hops[i].wait_recv()
            row_out[i] = product_narrow(whole[:, DK:], row_in[i]) + whole[:, :DK]
            hops[i].start()

        @pl.when(x == 3)
        def _():
            hops[i].wait_recv()

    def rows_of(i):
        for copy in z_copies[i]:
            copy.wait_recv()
        low = after(totals[i, 1], totals[i, 0])
        high = after(totals[i, 3], totals[i, 2])
        return low, after(high, low)

    def both_cores(i, low):
        none = jnp.concatenate([zero, ident], 1)
        third = after(totals[i, 2], low)
        head = jnp.where(
            z == 0, none, jnp.where(z == 1, totals[i, 0], jnp.where(z == 2, low, third))
        )
        return jnp.concatenate([head, after(early[i], head)], 0)

    quarter_rows = out_ref.shape[2]
    split = quarter_rows // 2
    gain = gain_ref[...]

    def relay(i, j):
        return remote(
            parcels.at[i, 1, pl.ds(j * split, split)], relays.at[i, j],
            r_send.at[i, j], r_recv.at[i, j], beside(1 + 2 * j),
        )

    def relayed(i, j):
        source = (group + 3 - 2 * j) % groups
        return remote(
            relays.at[i, j], out_ref.at[source, i, pl.ds(j * split, split)],
            p_send.at[i, j], p_recv.at[i, j], beside(1 + 2 * j),
        )

    def parcel(i, d):
        return remote(
            parcels.at[i, d - 1], out_ref.at[group, i], a_send.at[i, d // 2], a_recv.at[i, d // 2],
            beside(d),
        )

    backs = [
        remote(
            start_out.at[i], start_in.at[i], back_send.at[i], back_recv.at[i], {"seq": sibling}
        )
        for i in range(2)
    ]

    def states(i, both):
        state = product_narrow(both[:, DK:], row_in[i]) + both[:, :DK]
        start_out[i] = jnp.where(core == 0, state[DK:], state[:DK])
        backs[i].start()
        starts[mine + i] = jnp.where(core == 0, state[:DK], state[DK:])

    def emit(i):
        backs[i].wait_recv()
        starts[theirs + i] = start_in[i]
        for d in (2, 1, 3, 0):
            quarter = (group + d) % groups
            rows = pl.ds(pl.multiple_of(quarter * quarter_rows, quarter_rows), quarter_rows)
            for j in range(2):
                g = i + 2 * j
                piece = o_ref[g, rows, :]
                o = piece[:, :DK] + product_narrow(piece[:, DK:], starts[g])
                scale = lax.rsqrt(jnp.mean(o * o, -1, keepdims=True) + 1e-06)
                normed = (o * scale * gain).astype(BF16)
                if d == 0:
                    out_ref[group, i, :, j * DK : (j + 1) * DK] = normed
                else:
                    parcels[i, d - 1, :, j * DK : (j + 1) * DK] = normed
            if d == 2:
                relay(i, 0).start()
                relay(i, 1).start()
            elif d > 0:
                parcel(i, d).start()

    low0, whole0 = rows_of(0)
    pass_on(0, whole0)
    both0 = both_cores(0, low0)
    low1, whole1 = rows_of(1)
    states(0, both0)
    pass_on(1, whole1)
    both1 = both_cores(1, low1)
    emit(0)
    states(1, both1)
    for j in range(2):
        relay(0, j).wait_recv()
        relayed(0, j).start()
    emit(1)
    for j in range(2):
        relay(1, j).wait_recv()
        relayed(1, j).start()

    for i in range(2):
        for j in range(2):
            parcel(i, 1 + 2 * j).wait_recv()
            relayed(i, j).wait_recv()

    def sent(c, carry):
        for j in range(2):
            direct(c, 1 + 2 * j).wait_send()
            onward(c, j).wait_send()
        return carry

    lax.fori_loop(0, chunks, sent, 0)
    for i in range(2):
        pairs[i].wait_send()
        backs[i].wait_send()
        for copy in z_copies[i]:
            copy.wait_send()
        for j in range(2):
            relay(i, j).wait_send()
            relayed(i, j).wait_send()
            parcel(i, 1 + 2 * j).wait_send()

    @pl.when(x < 3)
    def _():
        for i in range(2):
            hops[i].wait_send()


def layer(x, w_query, w_key, w_value, beta_code, gain):
    tokens, depth = x.shape
    width = w_query.shape[1]
    groups = width // DK
    shares = lax.axis_size("heads")
    rows = tokens // shares
    chunks = tokens // CHUNK
    dma = pltpu.SemaphoreType.DMA
    vmem = pl.BlockSpec(memory_space=pltpu.VMEM)
    anywhere = pl.BlockSpec(memory_space=pl.ANY)
    return pl.pallas_call(
        layer_kernel,
        out_shape=jax.ShapeDtypeStruct((shares, 2, rows, width // 2), BF16),
        in_specs=[vmem, anywhere, anywhere, anywhere, vmem, vmem],
        out_specs=vmem,
        scratch_shapes=[
            pltpu.VMEM((3, shares * depth, width), BF16),
            pltpu.VMEM((shares - 1, tokens, depth), BF16),
            pltpu.VMEM((groups, DK, 2 * DK), F32),
            pltpu.VMEM((groups, tokens, 2 * DK), F32),
            pltpu.VMEM((2, DK, 2 * DK), F32),
            pltpu.VMEM((2, 4, DK, 2 * DK), F32),
            pltpu.VMEM((2, DK, DK), F32),
            pltpu.VMEM((2, DK, DK), F32),
            pltpu.VMEM((2, DK, DK), F32),
            pltpu.VMEM((2, DK, DK), F32),
            pltpu.VMEM((groups, DK, DK), F32),
            pltpu.VMEM((2, shares - 1, rows, width // 2), BF16),
            pltpu.VMEM((2, 2, rows // 2, width // 2), BF16),
            dma((3,)), dma((chunks, 2)), dma((chunks, 2)), dma((chunks, 2)), dma((chunks, 2)),
            dma((2,)), dma((2,)), dma((2,)), dma((2,)), dma((2, 3)), dma((2, 3)), dma((2,)), dma((2,)),
            dma((2, 2)), dma((2, 2)), dma((2, 2)), dma((2, 2)), dma((2, 2)), dma((2, 2)),
        ],
        compiler_params=pltpu.CompilerParams(
            collective_id=0, has_side_effects=True, vmem_limit_bytes=48 * 1024 * 1024
        ),
        cost_estimate=pl.CostEstimate(flops=40 * 10**9, bytes_accessed=64 << 20, transcendentals=0),
    )(x, w_query, w_key, w_value, beta_code, gain)


def out_kernel(y_ref, w_ref, out_ref):
    part = 0.0
    for i in range(2):
        w = jnp.concatenate([w_ref[0, pl.ds(i * DK, DK)], w_ref[0, pl.ds((i + 2) * DK, DK)]], 0)
        part += dot(y_ref[0, i], w)

    @pl.when(pl.program_id(0) == 0)
    def _():
        out_ref[...] = part

    @pl.when(pl.program_id(0) > 0)
    def _():
        out_ref[...] += part


def project_out(normed, w_out):
    shares, parts, rows, width = normed.shape
    return pl.pallas_call(
        out_kernel,
        grid=(shares,),
        out_shape=jax.ShapeDtypeStruct((rows, w_out.shape[2]), F32),
        in_specs=[
            pl.BlockSpec((1, parts, rows, width), lambda h: (h, 0, 0, 0)),
            pl.BlockSpec((1, parts * width, w_out.shape[2]), lambda h: (h, 0, 0)),
        ],
        out_specs=pl.BlockSpec((rows, w_out.shape[2]), lambda h: (0, 0)),
        compiler_params=pltpu.CompilerParams(vmem_limit_bytes=32 * 1024 * 1024),
    )(normed, w_out)


def whole_w_out(w_out):
    rows = w_out.shape[0] // lax.axis_size("seq")
    share = lax.dynamic_slice_in_dim(w_out, lax.axis_index("seq") * rows, rows, 0)
    return lax.all_gather(share, ("heads", "seq"), axis=0, tiled=True).reshape(
        lax.axis_size("heads"), w_out.shape[0], w_out.shape[1]
    )


def local(inputs, w_query, w_key, w_value, w_out, beta_code, gain):
    w_whole = whole_w_out(w_out)
    normed = layer(inputs, w_query, w_key, w_value, beta_code, gain.reshape(1, DK))
    return project_out(normed, w_whole)


def solution(mesh):
    in_specs = (
        P("seq", "heads"),
        P(None, "heads"),
        P(None, "heads"),
        P(None, "heads"),
        P("heads", None),
        P("seq", "heads"),
        P(),
    )
    out_specs = P(("seq", "heads"), None)
    return jax.shard_map(local, mesh=mesh, in_specs=in_specs, out_specs=out_specs, check_vma=False)
```

time: 199 us -> 131 us (0.66)
  waiting for transfers between devices: 46.3 us -> 0.04 us
  local copies, waits for them, and re-layouts: 29.5 us -> 11.8 us
  blocking collectives: 13.5 us -> 0 us
  Pallas kernels: 94.8 us -> 105 us
    all_gather x5 -> x1, waiting for transfers between devices: 44.4 us -> 0.02 us  [whole_w_out(): lax.all_gather(share, ('heads', 'seq'), axis=0, tiled=True)]
    unnamed x50 -> x13, local copies, waits for them, and re-layouts: 25.5 us -> 11.2 us
    all_gather x1 -> x0, blocking collectives: 13.5 us -> none  [whole_w_out(): across = lax.all_gather(share, 'heads', axis=0, tiled=False)]
    pallas_call x5 -> x1, Pallas kernels: 89.9 us -> 100 us  [layer(): pl.pallas_call(layer_kernel, out_shape=jax.ShapeDtypeStruct((shares, 2, r...]
    slice x2 -> x0, local copies, waits for them, and re-layouts: 3.09 us -> none  [the longest x1 2.35 us: local(): piece = lax.all_gather(inputs[part], 'heads', axis=0, tiled=False)]
  transfers between devices with their start and end apart: 5 -> 1, of which waited for: 4 -> 0; matrix products, arithmetic and copies ran while one was open for 2% -> 1% of each run, Pallas kernels for 45% -> 77%
where the time goes in v2:
time: 131 us; the launch traced here: 130 us
  Pallas kernels  105 us (80%)
  between operations  13.4 us (10%)
  local copies, waits for them, and re-layouts  11.8 us (9%)
    pallas_call x1, Pallas kernels, layer(): pl.pallas_call(layer_kernel, out_shape=jax.ShapeDtypeStruct((shares, 2, r...  100 us
    unnamed x13, local copies, waits for them, and re-layouts  11.2 us
    pallas_call x1, Pallas kernels, project_out(): pl.pallas_call(out_kernel, grid=(shares,), out_shape=jax.ShapeDtypeStruct...  4.88 us
  transfers between devices with their start and end apart: 1, of which 0 were waited for; matrix products, arithmetic and copies ran while one was open for 1% of the time, Pallas kernels for 77%

profile of v2, /device:TPU:6, one launch (start us, length us, event | category | flops | bytes accessed | tf_op | source)
XLA Modules:
  0.0 130.3 jit_solution(3096468738206832403)
XLA Ops:
  6.5 0.0 copy-start
  6.5 0.0 all-gather.2.cloned.1.call-start
  6.5 1.6 %copy-done = bf16[512,2048]{1,0:T(8,128)(2,1)S(1)} copy-done((bf16[512,2048]{1,0:T(8,128)(2,1)S(1)}, bf16[512,2048]{1,0:T(8,128)(2,1)}, u32[]{:S(2)}) %copy-start) | copy-done | bytes 2097176
  8.1 0.6 constant_dynamic-slice_fusion
  8.8 0.0 all-gather.2.cloned.1.call-update
  8.8 1.7 %copy.8.b_ref = s32[1024,4]{1,0:T(8,128)} copy(s32[1024,4]{0,1:T(4,128)} %param.12) | data formatting | bytes 32768 | tf_op args[5]
  10.5 0.0 copy-start.2
  10.5 1.0 copy-done.2
  11.6 0.0 copy-start.3
  11.6 1.6 %copy-done.3 = bf16[2048,512]{1,0:T(8,128)(2,1)S(1)} copy-done((bf16[2048,512]{1,0:T(8,128)(2,1)S(1)}, bf16[2048,512]{1,0:T(8,128)(2,1)}, u32[]{:S(2)}) %copy-start.3) | copy-done | bytes 2097176
  13.2 0.0 copy-start.4
  13.2 1.2 copy-done.4
  14.4 0.0 copy-start.5
  14.4 0.7 copy-done.5
  15.0 100.1 %shard_map.73.y_ref = bf16[4,2,256,256]{3,2,1,0:T(8,128)(2,1)S(1)} custom-call(bf16[1024,512]{1,0:T(8,128)(2,1)S(1)} %copy-done.4, bf16[2048,512]{1,0:T(8,128)(2,1)S(1)} %copy-done.3, bf16[2048,512]{1,0:T(8,128)(2,1)} %wk_hbm.1, bf16[2048,512]{1,0:T(8,128)(2,1)} %wv_hbm.1, s32[1024,4]{1,0:T(8,128)S(1)} %copy-done.2, f32[1,128]{1,0:T(1,128)S(1)} %bitcast.3), custom_call_target="tpu_custom_call" | custom-call | flops 40000000000 | bytes 67108864 | tf_op jit(solution)/shard_map/pallas_call | solution.py:403
  115.2 0.0 all-gather.2.cloned.1.call-done
  115.2 0.0 copy-start.1
  115.2 3.4 %copy-done.1 = bf16[2048,2048]{1,0:T(8,128)(2,1)S(1)} copy-done((bf16[2048,2048]{1,0:T(8,128)(2,1)S(1)}, bf16[2048,2048]{1,0:T(8,128)(2,1)}, u32[]{:S(2)}) %copy-start.1) | copy-done | bytes 8388632
  118.6 4.9 %shard_map.74 = f32[256,2048]{1,0:T(8,128)} custom-call(bf16[4,2,256,256]{3,2,1,0:T(8,128)(2,1)S(1)} %shard_map.73.y_ref, bf16[4,512,2048]{2,1,0:T(8,128)(2,1)S(1)} %bitcast.2), custom_call_target="tpu_custom_call" | custom-call | tf_op jit(solution)/shard_map/pallas_call | solution.py:450
Async XLA Ops:
  6.5 1.6 %copy-start = (bf16[512,2048]{1,0:T(8,128)(2,1)S(1)}, bf16[512,2048]{1,0:T(8,128)(2,1)}, u32[]{:S(2)}) copy-start(bf16[512,2048]{1,0:T(8,128)(2,1)} %param.11) | copy-start | bytes 6291460
  6.5 108.7 %all-gather.2.cloned.1.call-start = ((), (), s32[]{:S(2)}) async-start(), calls=%async_computation | async-start | bytes 8454144 | tf_op jit(solution)/shard_map/all_gather | solution.py:466
  10.5 1.0 copy-start.2
  11.6 1.6 %copy-start.3 = (bf16[2048,512]{1,0:T(8,128)(2,1)S(1)}, bf16[2048,512]{1,0:T(8,128)(2,1)}, u32[]{:S(2)}) copy-start(bf16[2048,512]{1,0:T(8,128)(2,1)} %wq_hbm.1) | copy-start | bytes 6291460
  13.2 1.2 copy-start.4
  14.4 0.7 copy-start.5
  115.2 3.4 %copy-start.1 = (bf16[2048,2048]{1,0:T(8,128)(2,1)S(1)}, bf16[2048,2048]{1,0:T(8,128)(2,1)}, u32[]{:S(2)}) copy-start(bf16[2048,2048]{1,0:T(8,128)(2,1)} %all-gather.2.cloned.1.call-done) | copy-start | bytes 25165828
Sparse Core Ops, SparseCore 0:
  10.3 79.6 all-gather.1

commit v3 on v2

--- a/solution.py
+++ b/solution.py
@@ -97,10 +97,12 @@
 
 
 def layer_kernel(
-    x_ref, wq_hbm, wk_hbm, wv_hbm, b_ref, gain_ref, out_ref,
-    w_ref, others, end_ref, o_ref,
-    sibling_end, totals, row_in, row_out, start_out, start_in, starts, parcels, relays,
-    w_sem, g_send, g_recv, f_send, f_recv,
+    x_hbm, wq_hbm, wk_hbm, wv_hbm, wo_hbm, b_hbm, gain_hbm, out_ref,
+    x_ref, b_ref, gain_ref, w_ref, wo_ref, others, end_ref, o_ref,
+    sibling_end, totals, row_in, row_out, start_out, start_in, starts, parcels, relays, got,
+    w_sem, l_sem, g_send, g_recv, f_send, f_recv,
+    across_send, across_recv, first_send, first_recv, second_send, second_recv,
+    third_send, third_recv, fourth_send, fourth_recv,
     pair_send, pair_recv, back_send, back_recv, z_send, z_recv, x_send, x_recv,
     a_send, a_recv, r_send, r_recv, p_send, p_recv,
 ):
@@ -134,20 +136,106 @@
     for d in range(1, 4):
         greet(at(x, (z + d) % 4, core))
         greet(beside(d))
-    greet(at((x + 1) % 4, z, core))
-    greet(at((x + 3) % 4, z, core))
+        greet(at((x + d) % 4, z, core))
     loads = [
         pltpu.make_async_copy(w, w_ref.at[i], w_sem.at[i])
         for i, w in enumerate((wq_hbm, wk_hbm, wv_hbm))
     ]
     for load in loads:
         load.start()
-    pl.semaphore_wait(barrier, 9)
+    smalls = [
+        pltpu.make_async_copy(x_hbm, x_ref, l_sem.at[0]),
+        pltpu.make_async_copy(b_hbm, b_ref, l_sem.at[1]),
+        pltpu.make_async_copy(gain_hbm, gain_ref, l_sem.at[2]),
+    ]
+    for load in smalls:
+        load.start()
+    pl.semaphore_wait(barrier, 10)
+
+    across = [
+        remote(
+            wo_hbm.at[x, z, core], wo_ref.at[d, x, z, core],
+            across_send.at[d - 1], across_recv.at[d - 1], beside(d),
+        )
+        for d in (1, 3, 2)
+    ]
+    back = pl.ds(1, 3)
+
+    def along(core_now, first, d):
+        if (core_now == 0) == first:
+            return at(x, (z + d) % 4, core)
+        return at((x + d) % 4, z, core)
+
+    def firsts(core_now):
+        return [
+            remote(
+                wo_ref.at[back, x, z, core_now], wo_ref.at[back, x, z, core_now],
+                first_send.at[d - 1], first_recv.at[d - 1], along(core_now, True, d),
+            )
+            for d in (1, 3, 2)
+        ]
+
+    def line(core_now, place):
+        if core_now == 0:
+            return wo_ref.at[back, place, :, 0]
+        return wo_ref.at[back, :, place, 1]
+
+    def seconds(core_now):
+        here = line(core_now, x if core_now == 0 else z)
+        return [
+            remote(
+                here, here, second_send.at[d // 2], second_recv.at[d // 2],
+                along(core_now, False, d),
+            )
+            for d in (1, 3)
+        ]
+
+    def half_line(core_now, place, j):
+        if core_now == 0:
+            return wo_ref.at[back, place, pl.ds(2 * j, 2), 0]
+        return wo_ref.at[back, pl.ds(2 * j, 2), place, 1]
+
+    def thirds(core_now):
+        place = x if core_now == 0 else z
+        return [
+            remote(
+                half_line(core_now, (place + 3 - 2 * j) % 4, j),
+                half_line(core_now, (place + 3 - 2 * j) % 4, j),
+                third_send.at[j], third_recv.at[j], along(core_now, False, 1 + 2 * j),
+            )
+            for j in range(2)
+        ]
+
+    def fourth():
+        here = wo_ref.at[back, :, :, core]
+        return remote(here, here, fourth_send.at[0], fourth_recv.at[0], {"seq": sibling})
+
+    def either(do):
+        for core_now in range(2):
+            @pl.when(core == core_now)
+            def _():
+                do(core_now)
+
+    def begin(copies):
+        for copy in copies:
+            copy.start()
+
+    def arrived(copies):
+        for copy in copies:
+            copy.wait_recv()
+
+    def left(copies):
+        for copy in copies:
+            copy.wait_send()
+
+    begin(across)
+    own_w = [pltpu.make_async_copy(wo_hbm, wo_ref.at[0], l_sem.at[3])]
+    begin(own_w)
 
     def direct(c, d):
         rows = pl.ds(pl.multiple_of(c * CHUNK, CHUNK), CHUNK)
         return remote(
-            x_ref.at[rows], others.at[d - 1, rows], g_send.at[c, d // 2], g_recv.at[c, d // 2],
+            x_hbm.at[rows], others.at[d - 1, rows], g_send.at[c, d // 2], g_recv.at[c, d // 2],
             beside(d),
         )
 
@@ -175,9 +263,11 @@
     zero = jnp.zeros((DK, DK), F32)
     for h in range(end_ref.shape[0]):
         end_ref[h] = jnp.concatenate([zero, ident], 1)
+    arrived(across)
+    either(lambda core_now: begin(firsts(core_now)))
     start_onward(0)
     start_direct(2)
-    for load in loads:
+    for load in loads + smalls:
         load.wait()
 
     def step(c, carry):
@@ -201,7 +291,28 @@
         def _():
             start_direct(c + 3)
 
-        strength = b_ref[rows, :].astype(F32) * (1.0 / 64.0)
+        @pl.when(c == 0)
+        def _():
+            def go(core_now):
+                arrived(firsts(core_now))
+                begin(seconds(core_now))
+
+            either(go)
+
+        @pl.when(c == 1)
+        def _():
+            def go(core_now):
+                arrived(seconds(core_now))
+                begin(thirds(core_now))
+
+            either(go)
+
+        @pl.when(c == 2)
+        def _():
+            either(lambda core_now: arrived(thirds(core_now)))
+            fourth().start()
+
+        strength = (b_ref[:, rows].astype(F32) * (1.0 / 64.0)).T
         scan_chunk(
             query, keys, values, strength, end_ref, o_ref, pl.multiple_of(c * CHUNK, CHUNK)
         )
@@ -240,14 +351,14 @@
         z_copies.append(
             [
                 remote(
-                    totals.at[i, z], totals.at[i, z], z_send.at[i, d - 1], z_recv.at[i, d - 1],
+                    totals.at[i, z], totals.at[i, z], z_send.at[i, d // 2], z_recv.at[i, d // 2],
                     at(x, (z + d) % 4, core),
                 )
-                for d in (1, 3, 2)
+                for d in (1, 3)
             ]
         )
-        for copy in z_copies[i]:
-            copy.start()
+        if i == 0:
+            begin(z_copies[i])
 
     hops = [
         remote(
@@ -256,12 +367,13 @@
         for i in range(2)
     ]
 
-    def pass_on(i, whole):
+    def set_out(i, whole):
         @pl.when(x == 0)
         def _():
             row_out[i] = whole[:, :DK]
             hops[i].start()
 
+    def pass_on(i, whole):
         @pl.when(jnp.logical_and(x > 0, x < 3))
         def _():
             hops[i].wait_recv()
@@ -272,9 +384,18 @@
         def _():
             hops[i].wait_recv()
 
+    def z_onward(i):
+        return [
+            remote(
+                totals.at[i, (z + 3 - 2 * j) % 4, pl.ds(j * (DK // 2), DK // 2)],
+                totals.at[i, (z + 3 - 2 * j) % 4, pl.ds(j * (DK // 2), DK // 2)],
+                z_send.at[i, 2 + j], z_recv.at[i, 2 + j], at(x, (z + 1 + 2 * j) % 4, core),
+            )
+            for j in range(2)
+        ]
+
     def rows_of(i):
-        for copy in z_copies[i]:
-            copy.wait_recv()
+        arrived(z_onward(i))
         low = after(totals[i, 1], totals[i, 0])
         high = after(totals[i, 3], totals[i, 2])
         return low, after(high, low)
@@ -287,7 +408,7 @@
         )
         return jnp.concatenate([head, after(early[i], head)], 0)
 
-    quarter_rows = out_ref.shape[2]
+    quarter_rows = got.shape[2]
     split = quarter_rows // 2
     gain = gain_ref[...]
 
@@ -298,15 +419,14 @@
         )
 
     def relayed(i, j):
-        source = (group + 3 - 2 * j) % groups
         return remote(
-            relays.at[i, j], out_ref.at[source, i, pl.ds(j * split, split)],
+            relays.at[i, j], got.at[2, i, pl.ds(j * split, split)],
             p_send.at[i, j], p_recv.at[i, j], beside(1 + 2 * j),
         )
 
     def parcel(i, d):
         return remote(
-            parcels.at[i, d - 1], out_ref.at[group, i], a_send.at[i, d // 2], a_recv.at[i, d // 2],
+            parcels.at[i, d - 1], got.at[d, i], a_send.at[i, d // 2], a_recv.at[i, d // 2],
             beside(d),
         )
 
@@ -336,7 +456,7 @@
                 scale = lax.rsqrt(jnp.mean(o * o, -1, keepdims=True) + 1e-06)
                 normed = (o * scale * gain).astype(BF16)
                 if d == 0:
-                    out_ref[group, i, :, j * DK : (j + 1) * DK] = normed
+                    got[0, i, :, j * DK : (j + 1) * DK] = normed
                 else:
                     parcels[i, d - 1, :, j * DK : (j + 1) * DK] = normed
             if d == 2:
@@ -345,27 +465,60 @@
             elif d > 0:
                 parcel(i, d).start()
 
+    columns = out_ref.shape[1]
+    tile = 512
+
+    def mix(i, d, first=False):
+        def one(n, carry):
+            lanes = pl.ds(pl.multiple_of(n * tile, tile), tile)
+            w = [
+                wo_ref[d, i + 2 * j, :, :, :, lanes].reshape(DK, tile)
+                for j in range(2)
+            ]
+            part = dot(got[d, i], jnp.concatenate(w, 0))
+            if first:
+                out_ref[:, lanes] = part
+            else:
+                out_ref[:, lanes] += part
+            return carry
+
+        lax.fori_loop(0, columns // tile, one, 0)
+
+    arrived(z_copies[0])
+    begin(z_onward(0))
+    begin(z_copies[1])
     low0, whole0 = rows_of(0)
+    set_out(0, whole0)
+    both0 = both_cores(0, low0)
+    arrived(z_copies[1])
+    begin(z_onward(1))
     pass_on(0, whole0)
-    both0 = both_cores(0, low0)
+    states(0, both0)
     low1, whole1 = rows_of(1)
-    states(0, both0)
-    pass_on(1, whole1)
+    set_out(1, whole1)
     both1 = both_cores(1, low1)
     emit(0)
+    pass_on(1, whole1)
     states(1, both1)
     for j in range(2):
         relay(0, j).wait_recv()
         relayed(0, j).start()
+    fourth().wait_recv()
+    for load in own_w:
+        load.wait()
+    mix(0, 0, True)
     emit(1)
     for j in range(2):
         relay(1, j).wait_recv()
         relayed(1, j).start()
-
+    mix(1, 0)
     for i in range(2):
-        for j in range(2):
-            parcel(i, 1 + 2 * j).wait_recv()
-            relayed(i, j).wait_recv()
+        for d in (1, 3):
+            parcel(i, d).wait_recv()
+            mix(i, d)
+        relayed(i, 0).wait_recv()
+        relayed(i, 1).wait_recv()
+        mix(i, 2)
 
     def sent(c, carry):
         for j in range(2):
@@ -374,11 +527,13 @@
         return carry
 
     lax.fori_loop(0, chunks, sent, 0)
+    left(across)
+    either(lambda core_now: left(firsts(core_now) + seconds(core_now) + thirds(core_now)))
+    left([fourth()])
     for i in range(2):
         pairs[i].wait_send()
         backs[i].wait_send()
-        for copy in z_copies[i]:
-            copy.wait_send()
+        left(z_copies[i] + z_onward(i))
         for j in range(2):
             relay(i, j).wait_send()
             relayed(i, j).wait_send()
@@ -390,23 +545,29 @@
             hops[i].wait_send()
 
 
-def layer(x, w_query, w_key, w_value, beta_code, gain):
-    tokens, depth = x.shape
+def local(inputs, w_query, w_key, w_value, w_out, beta_code, gain):
+    tokens, depth = inputs.shape
     width = w_query.shape[1]
     groups = width // DK
     shares = lax.axis_size("heads")
+    shards = lax.axis_size("seq")
     rows = tokens // shares
     chunks = tokens // CHUNK
+    columns = w_out.shape[1]
+    w_parts = w_out.reshape(4, 4, 2, width // shards, columns)
     dma = pltpu.SemaphoreType.DMA
-    vmem = pl.BlockSpec(memory_space=pltpu.VMEM)
     anywhere = pl.BlockSpec(memory_space=pl.ANY)
     return pl.pallas_call(
         layer_kernel,
-        out_shape=jax.ShapeDtypeStruct((shares, 2, rows, width // 2), BF16),
-        in_specs=[vmem, anywhere, anywhere, anywhere, vmem, vmem],
-        out_specs=vmem,
+        out_shape=jax.ShapeDtypeStruct((rows, columns), F32),
+        in_specs=[anywhere] * 7,
+        out_specs=pl.BlockSpec(memory_space=pltpu.VMEM),
         scratch_shapes=[
+            pltpu.VMEM((tokens, depth), BF16),
+            pltpu.VMEM((groups, tokens), jnp.int32),
+            pltpu.VMEM((1, DK), F32),
             pltpu.VMEM((3, shares * depth, width), BF16),
+            pltpu.VMEM((shares, 4, 4, 2, width // shards, columns), BF16),
             pltpu.VMEM((shares - 1, tokens, depth), BF16),
             pltpu.VMEM((groups, DK, 2 * DK), F32),
             pltpu.VMEM((groups, tokens, 2 * DK), F32),
@@ -419,59 +580,19 @@
             pltpu.VMEM((groups, DK, DK), F32),
             pltpu.VMEM((2, shares - 1, rows, width // 2), BF16),
             pltpu.VMEM((2, 2, rows // 2, width // 2), BF16),
-            dma((3,)), dma((chunks, 2)), dma((chunks, 2)), dma((chunks, 2)), dma((chunks, 2)),
-            dma((2,)), dma((2,)), dma((2,)), dma((2,)), dma((2, 3)), dma((2, 3)), dma((2,)), dma((2,)),
+            pltpu.VMEM((shares, 2, rows, width // 2), BF16),
+            dma((3,)), dma((4,)),
+            dma((chunks, 2)), dma((chunks, 2)), dma((chunks, 2)), dma((chunks, 2)),
+            dma((3,)), dma((3,)), dma((3,)), dma((3,)), dma((2,)), dma((2,)),
+            dma((2,)), dma((2,)), dma((1,)), dma((1,)),
+            dma((2,)), dma((2,)), dma((2,)), dma((2,)), dma((2, 4)), dma((2, 4)), dma((2,)), dma((2,)),
             dma((2, 2)), dma((2, 2)), dma((2, 2)), dma((2, 2)), dma((2, 2)), dma((2, 2)),
         ],
         compiler_params=pltpu.CompilerParams(
-            collective_id=0, has_side_effects=True, vmem_limit_bytes=48 * 1024 * 1024
+            collective_id=0, has_side_effects=True, vmem_limit_bytes=60 * 1024 * 1024
         ),
         cost_estimate=pl.CostEstimate(flops=40 * 10**9, bytes_accessed=64 << 20, transcendentals=0),
-    )(x, w_query, w_key, w_value, beta_code, gain)
-
-
-def out_kernel(y_ref, w_ref, out_ref):
-    part = 0.0
-    for i in range(2):
-        w = jnp.concatenate([w_ref[0, pl.ds(i * DK, DK)], w_ref[0, pl.ds((i + 2) * DK, DK)]], 0)
-        part += dot(y_ref[0, i], w)
-
-    @pl.when(pl.program_id(0) == 0)
-    def _():
-        out_ref[...] = part
-
-    @pl.when(pl.program_id(0) > 0)
-    def _():
-        out_ref[...] += part
-
-
-def project_out(normed, w_out):
-    shares, parts, rows, width = normed.shape
-    return pl.pallas_call(
-        out_kernel,
-        grid=(shares,),
-        out_shape=jax.ShapeDtypeStruct((rows, w_out.shape[2]), F32),
-        in_specs=[
-            pl.BlockSpec((1, parts, rows, width), lambda h: (h, 0, 0, 0)),
-            pl.BlockSpec((1, parts * width, w_out.shape[2]), lambda h: (h, 0, 0)),
-        ],
-        out_specs=pl.BlockSpec((rows, w_out.shape[2]), lambda h: (0, 0)),
-        compiler_params=pltpu.CompilerParams(vmem_limit_bytes=32 * 1024 * 1024),
-    )(normed, w_out)
-
-
-def whole_w_out(w_out):
-    rows = w_out.shape[0] // lax.axis_size("seq")
-    share = lax.dynamic_slice_in_dim(w_out, lax.axis_index("seq") * rows, rows, 0)
-    return lax.all_gather(share, ("heads", "seq"), axis=0, tiled=True).reshape(
-        lax.axis_size("heads"), w_out.shape[0], w_out.shape[1]
-    )
-
-
-def local(inputs, w_query, w_key, w_value, w_out, beta_code, gain):
-    w_whole = whole_w_out(w_out)
-    normed = layer(inputs, w_query, w_key, w_value, beta_code, gain.reshape(1, DK))
-    return project_out(normed, w_whole)
+    )(inputs, w_query, w_key, w_value, w_parts, beta_code.T, gain.reshape(1, DK))
 
 
 def solution(mesh):

time: 131 us -> 101 us (0.77)
  between operations: 13.4 us -> 0.01 us
  local copies, waits for them, and re-layouts: 11.8 us -> 3.14 us
  Pallas kernels: 105 us -> 98.1 us
    unnamed x13 -> x1, local copies, waits for them, and re-layouts: 11.2 us -> 3.14 us
    pallas_call x2 -> x1, Pallas kernels: 105 us -> 98.1 us  [local(): pl.pallas_call(layer_kernel, out_shape=jax.ShapeDtypeStruct((rows, column...]
  transfers between devices with their start and end apart: 1 -> 0, of which waited for: 0 -> 0; matrix products, arithmetic and copies ran while one was open for 1% -> 0% of each run, Pallas kernels for 77% -> 0%
where the time goes in v3:
time: 101 us
  Pallas kernels  98.1 us (97%)
  local copies, waits for them, and re-layouts  3.14 us (3%)
    pallas_call x1, Pallas kernels, local(): pl.pallas_call(layer_kernel, out_shape=jax.ShapeDtypeStruct((rows, column...  98.1 us
    unnamed x1, local copies, waits for them, and re-layouts  3.14 us

profile of v3, /device:TPU:6, one launch (start us, length us, event | category | flops | bytes accessed | tf_op | source)
XLA Modules:
  0.0 101.2 jit_solution(7129235657218648419)
XLA Ops:
  0.0 98.1 %shard_map.73 = f32[256,2048]{1,0:T(8,128)} custom-call(bf16[1024,512]{1,0:T(8,128)(2,1)} %x_hbm.1, bf16[2048,512]{1,0:T(8,128)(2,1)} %wq_hbm.1, bf16[2048,512]{1,0:T(8,128)(2,1)} %wk_hbm.1, bf16[2048,512]{1,0:T(8,128)(2,1)} %wv_hbm.1, bf16[4,4,2,16,2048]{4,3,2,1,0:T(8,128)(2,1)} %bitcast.3, s32[4,1024]{1,0:T(4,128)} %bitcast.4, f32[1,128]{1,0:T(1,128)} %bitcast.5), custom_call_target="tpu_custom_call" | custom-call | flops 40000000000 | bytes 67108864 | tf_op jit(solution)/shard_map/pallas_call | solution.py:560
  98.1 3.1 %copy.9 = f32[256,2048]{1,0:T(8,128)} copy(f32[256,2048]{1,0:T(8,128)} %shard_map.73) | data formatting | bytes 4194304

commit v4 on v3

--- a/solution.py
+++ b/solution.py
@@ -99,12 +99,12 @@
 def layer_kernel(
     x_hbm, wq_hbm, wk_hbm, wv_hbm, wo_hbm, b_hbm, gain_hbm, out_ref,
     x_ref, b_ref, gain_ref, w_ref, wo_ref, others, end_ref, o_ref,
-    sibling_end, totals, row_in, row_out, start_out, start_in, starts, parcels, relays, got,
+    sibling_end, totals, row_in, row_out, start_out, start_in, starts, parcels, got,
     w_sem, l_sem, g_send, g_recv, f_send, f_recv,
     across_send, across_recv, first_send, first_recv, second_send, second_recv,
     third_send, third_recv, fourth_send, fourth_recv,
     pair_send, pair_recv, back_send, back_recv, z_send, z_recv, x_send, x_recv,
-    a_send, a_recv, r_send, r_recv, p_send, p_recv,
+    a_send, a_recv,
 ):
     group = lax.axis_index("heads")
     me = lax.axis_index("seq")
@@ -141,14 +141,12 @@
         pltpu.make_async_copy(w, w_ref.at[i], w_sem.at[i])
         for i, w in enumerate((wq_hbm, wk_hbm, wv_hbm))
     ]
-    for load in loads:
-        load.start()
     smalls = [
         pltpu.make_async_copy(x_hbm, x_ref, l_sem.at[0]),
         pltpu.make_async_copy(b_hbm, b_ref, l_sem.at[1]),
         pltpu.make_async_copy(gain_hbm, gain_ref, l_sem.at[2]),
     ]
-    for load in smalls:
+    for load in smalls + loads:
         load.start()
     pl.semaphore_wait(barrier, 10)
 
@@ -235,7 +233,7 @@
     def direct(c, d):
         rows = pl.ds(pl.multiple_of(c * CHUNK, CHUNK), CHUNK)
         return remote(
-            x_hbm.at[rows], others.at[d - 1, rows], g_send.at[c, d // 2], g_recv.at[c, d // 2],
+            x_ref.at[rows], others.at[d - 1, rows], g_send.at[c, d // 2], g_recv.at[c, d // 2],
             beside(d),
         )
 
@@ -256,6 +254,7 @@
         onward(c, 0).start()
         onward(c, 1).start()
 
+    smalls[0].wait()
     start_direct(0)
     start_direct(1)
     row, col = iotas()
@@ -267,7 +266,7 @@
     either(lambda core_now: begin(firsts(core_now)))
     start_onward(0)
     start_direct(2)
-    for load in loads + smalls:
+    for load in loads + smalls[1:]:
         load.wait()
 
     def step(c, carry):
@@ -409,24 +408,11 @@
         return jnp.concatenate([head, after(early[i], head)], 0)
 
     quarter_rows = got.shape[2]
-    split = quarter_rows // 2
     gain = gain_ref[...]
-
-    def relay(i, j):
-        return remote(
-            parcels.at[i, 1, pl.ds(j * split, split)], relays.at[i, j],
-            r_send.at[i, j], r_recv.at[i, j], beside(1 + 2 * j),
-        )
-
-    def relayed(i, j):
-        return remote(
-            relays.at[i, j], got.at[2, i, pl.ds(j * split, split)],
-            p_send.at[i, j], p_recv.at[i, j], beside(1 + 2 * j),
-        )
 
     def parcel(i, d):
         return remote(
-            parcels.at[i, d - 1], got.at[d, i], a_send.at[i, d // 2], a_recv.at[i, d // 2],
+            parcels.at[i, d - 1], got.at[d, i], a_send.at[i, d - 1], a_recv.at[i, d - 1],
             beside(d),
         )
 
@@ -459,14 +445,11 @@
                     got[0, i, :, j * DK : (j + 1) * DK] = normed
                 else:
                     parcels[i, d - 1, :, j * DK : (j + 1) * DK] = normed
-            if d == 2:
-                relay(i, 0).start()
-                relay(i, 1).start()
-            elif d > 0:
+            if d > 0:
                 parcel(i, d).start()
 
     columns = out_ref.shape[1]
-    tile = 512
+    tile = columns
 
     def mix(i, d, first=False):
         def one(n, carry):
@@ -500,25 +483,16 @@
     emit(0)
     pass_on(1, whole1)
     states(1, both1)
-    for j in range(2):
-        relay(0, j).wait_recv()
-        relayed(0, j).start()
     fourth().wait_recv()
     for load in own_w:
         load.wait()
     mix(0, 0, True)
     emit(1)
-    for j in range(2):
-        relay(1, j).wait_recv()
-        relayed(1, j).start()
     mix(1, 0)
     for i in range(2):
-        for d in (1, 3):
+        for d in (1, 3, 2):
             parcel(i, d).wait_recv()
             mix(i, d)
-        relayed(i, 0).wait_recv()
-        relayed(i, 1).wait_recv()
-        mix(i, 2)
 
     def sent(c, carry):
         for j in range(2):
@@ -534,10 +508,7 @@
         pairs[i].wait_send()
         backs[i].wait_send()
         left(z_copies[i] + z_onward(i))
-        for j in range(2):
-            relay(i, j).wait_send()
-            relayed(i, j).wait_send()
-            parcel(i, 1 + 2 * j).wait_send()
+        left([parcel(i, d) for d in (1, 3, 2)])
 
     @pl.when(x < 3)
     def _():
@@ -579,14 +550,13 @@
             pltpu.VMEM((2, DK, DK), F32),
             pltpu.VMEM((groups, DK, DK), F32),
             pltpu.VMEM((2, shares - 1, rows, width // 2), BF16),
-            pltpu.VMEM((2, 2, rows // 2, width // 2), BF16),
             pltpu.VMEM((shares, 2, rows, width // 2), BF16),
             dma((3,)), dma((4,)),
             dma((chunks, 2)), dma((chunks, 2)), dma((chunks, 2)), dma((chunks, 2)),
             dma((3,)), dma((3,)), dma((3,)), dma((3,)), dma((2,)), dma((2,)),
             dma((2,)), dma((2,)), dma((1,)), dma((1,)),
             dma((2,)), dma((2,)), dma((2,)), dma((2,)), dma((2, 4)), dma((2, 4)), dma((2,)), dma((2,)),
-            dma((2, 2)), dma((2, 2)), dma((2, 2)), dma((2, 2)), dma((2, 2)), dma((2, 2)),
+            dma((2, 3)), dma((2, 3)),
         ],
         compiler_params=pltpu.CompilerParams(
             collective_id=0, has_side_effects=True, vmem_limit_bytes=60 * 1024 * 1024

time: 101 us -> 100 us (0.990)
  Pallas kernels: 98.1 us -> 96.6 us
    pallas_call x1, Pallas kernels: 98.1 us -> 96.6 us  [local(): pl.pallas_call(layer_kernel, out_shape=jax.ShapeDtypeStruct((rows, column...]
where the time goes in v4:
time: 100 us; the launch traced here: 99.7 us
  Pallas kernels  96.6 us (97%)
  local copies, waits for them, and re-layouts  3.14 us (3%)
    pallas_call x1, Pallas kernels, local(): pl.pallas_call(layer_kernel, out_shape=jax.ShapeDtypeStruct((rows, column...  96.6 us
    unnamed x1, local copies, waits for them, and re-layouts  3.14 us

profile of v4, /device:TPU:6, one launch (start us, length us, event | category | flops | bytes accessed | tf_op | source)
XLA Modules:
  0.0 99.7 jit_solution(7990756379312102934)
XLA Ops:
  0.0 96.6 %shard_map.73 = f32[256,2048]{1,0:T(8,128)} custom-call(bf16[1024,512]{1,0:T(8,128)(2,1)} %x_hbm.1, bf16[2048,512]{1,0:T(8,128)(2,1)} %wq_hbm.1, bf16[2048,512]{1,0:T(8,128)(2,1)} %wk_hbm.1, bf16[2048,512]{1,0:T(8,128)(2,1)} %wv_hbm.1, bf16[4,4,2,16,2048]{4,3,2,1,0:T(8,128)(2,1)} %bitcast.3, s32[4,1024]{1,0:T(4,128)} %bitcast.4, f32[1,128]{1,0:T(1,128)} %bitcast.5), custom_call_target="tpu_custom_call" | custom-call | flops 40000000000 | bytes 67108864 | tf_op jit(solution)/shard_map/pallas_call | solution.py:531
  96.6 3.1 %copy.9 = f32[256,2048]{1,0:T(8,128)} copy(f32[256,2048]{1,0:T(8,128)} %shard_map.73) | data formatting | bytes 4194304
